TPU v7x, 512 devices: a whole 4x8x8 slice. The times are simulated.
512 devices in a mesh: branch: 2 (over y_hi), trow: 8 (over z), tcol: 32 (over x, y_lo, core).
Axes of the slice: x: 4, y: 8 (y_hi: 2, y_lo: 4; y = y_hi * 4 + y_lo), z: 8, core: 2. Of those that a mesh axis runs over, the one named last changes fastest.
Arguments:
- latent: bfloat16 [2, 2, 64, 256, 1152], P('branch', None, 'trow', 'tcol'), may hold values from -6 to 6
- modulation: float32 [2, 3, 1152], replicated, may hold values from -2 to 2
- w_query: bfloat16 [2, 1152, 576], P('branch', None, 'tcol'), may hold values from -0.176776695 to 0.176776695
- w_keyval: bfloat16 [2, 1152, 1152], P('branch', None, 'tcol'), may hold values from -3.8301617 to 3.8301617
- w_out: bfloat16 [2, 576, 1152], P('branch', 'tcol'), may hold values from -0.25 to 0.25
- w_zero: bfloat16 [1152, 1152], P(None, 'tcol'), may hold values from -0.1875 to 0.1875
Outputs:
- hidden_out: bfloat16 [2, 2, 64, 256, 1152], P('branch', None, 'trow', 'tcol')
All inputs are finite; a program needn't handle non-finite values.
Results may differ from a plain program's by a relative error of at most 0.0075.
Values may be sent and summed in bfloat16 or wider, within the bound.
A program may use at most 128 MiB of HBM per device.

v0:
```python
import math
import jax
import jax.numpy as jnp
from jax import lax
from jax.sharding import PartitionSpec as P

D = 1152
HD = 72
HEADS = 8
WIN = 13
HW = 576


def padded(block, sides, width):
    for axis, dim in sides:
        count = lax.axis_size(axis)
        forward = [(i, i + 1) for i in range(count - 1)]
        backward = [(target, source) for source, target in forward]
        low = lax.ppermute(
            lax.slice_in_dim(block, block.shape[dim] - width, None, axis=dim), axis, forward
        )
        high = lax.ppermute(lax.slice_in_dim(block, 0, width, axis=dim), axis, backward)
        block = jnp.concatenate([low, block, high], axis=dim)
    return block


def shifted(block, axis, distance):
    devices = range(lax.axis_size(axis))
    route = [(i - distance, i) for i in devices if i - distance in devices]
    return lax.ppermute(block, axis, route)


def modulate(hidden, shift_scale):
    average = jnp.mean(hidden, axis=-1, keepdims=True)
    centred = hidden - average
    variance = jnp.mean(centred * centred, axis=-1, keepdims=True)
    return (centred * lax.rsqrt(variance + 1e-06) * (1.0 + shift_scale[1]) + shift_scale[0]).astype(
        jnp.bfloat16
    )


def block_mask(row_first, col_first, total_rows, total_cols, key_count):
    query_edge = 8
    radius = WIN // 2
    key_side = query_edge + 2 * radius
    offsets = jnp.arange(query_edge)
    reaches = jnp.arange(key_side)
    row_starts = jnp.clip(row_first + offsets - radius, 0, total_rows - WIN)
    key_rows = row_first - radius + reaches
    row_inside = (key_rows[None, :] >= row_starts[:, None]) & (
        key_rows[None, :] < row_starts[:, None] + WIN
    )
    col_starts = jnp.clip(col_first + offsets - radius, 0, total_cols - WIN)
    key_cols = col_first - radius + reaches
    col_inside = (key_cols[None, :] >= col_starts[:, None]) & (
        key_cols[None, :] < col_starts[:, None] + WIN
    )
    joined = row_inside[:, None, :, None] & col_inside[None, :, None, :]
    joined = joined.reshape(query_edge * query_edge, key_side * key_side)
    filler = jnp.zeros((query_edge * query_edge, key_count - key_side * key_side), dtype=jnp.bool_)
    return jnp.concatenate([joined, filler], axis=1)


def edge_keys(key_values):
    radius = WIN // 2
    return padded(key_values, (("trow", 1), ("tcol", 2)), radius)


def attend_tile(queries, extended, row_anchor, col_anchor, total_rows, total_cols):
    images, tile_rows, tile_cols = (queries.shape[0], queries.shape[1], queries.shape[2])
    query_edge = 8
    radius = WIN // 2
    key_side = query_edge + 2 * radius
    key_count = (key_side * key_side + 127) // 128 * 128
    across = tile_cols // query_edge
    block_count = tile_rows // query_edge * across
    scaling = 1.0 / math.sqrt(HD)

    def one_block(position):
        row_block = position // across * query_edge
        col_block = position % across * query_edge
        query_block = queries
        query_block = query_block.reshape(images, query_edge * query_edge, HEADS, HD)
        key_block = extended
        key_block = key_block.reshape(images, key_side * key_side, 2 * HW)
        key_block = jnp.pad(key_block, ((0, 0), (0, key_count - key_side * key_side), (0, 0)))
        key_heads = key_block[..., :HW].reshape(images, key_count, HEADS, HD)
        value_heads = key_block[..., HW:].reshape(images, key_count, HEADS, HD)
        allowed = block_mask(
            row_anchor + row_block, col_anchor + col_block, total_rows, total_cols, key_count
        )
        scores = (
            jnp.einsum(
                "iqhd,ikhd->ihqk", query_block, key_heads, preferred_element_type=jnp.float32
            )
            * scaling
        )
        scores = jnp.where(allowed[None, None], scores, -1e30)
        highest = jnp.max(scores, axis=-1, keepdims=True)
        raised = jnp.exp(scores - highest)
        totals = jnp.sum(raised, axis=-1, keepdims=True)
        weights = (raised / totals).astype(jnp.bfloat16)
        blended = jnp.einsum(
            "ihqk,ikhd->iqhd", weights, value_heads, preferred_element_type=jnp.float32
        )
        return blended.astype(jnp.bfloat16).reshape(images, query_edge, query_edge, HW)

    result = lax.map(one_block, jnp.arange(block_count))
    result = result.reshape(tile_rows // query_edge, across, images, query_edge, query_edge, HW)
    return result.transpose(2, 0, 3, 1, 4, 5).reshape(images, tile_rows, tile_cols, HW)


def run_block(active, hidden, shift_scale, weight_q, weight_kv, weight_o):
    images, tile_rows, tile_cols = (hidden.shape[0], hidden.shape[1], hidden.shape[2])
    tokens = images * tile_rows * tile_cols

    def project():
        flattened = modulate(hidden, shift_scale).reshape(tokens, D)
        queries = jnp.dot(flattened, weight_q, preferred_element_type=jnp.float32).astype(
            jnp.bfloat16
        )
        key_values = jnp.dot(flattened, weight_kv, preferred_element_type=jnp.float32).astype(
            jnp.bfloat16
        )
        return (queries, key_values)

    def nothing():
        return (jnp.zeros((tokens, HW), jnp.bfloat16), jnp.zeros((tokens, 2 * HW), jnp.bfloat16))

    queries, key_values = lax.cond(active, project, nothing)
    extended = edge_keys(key_values.reshape(images, tile_rows, tile_cols, 2 * HW))
    row_anchor = lax.axis_index("trow") * tile_rows
    col_anchor = lax.axis_index("tcol") * tile_cols
    total_rows = tile_rows * lax.axis_size("trow")
    total_cols = tile_cols * lax.axis_size("tcol")

    def finish():
        attended = attend_tile(
            queries.reshape(images, tile_rows, tile_cols, HW),
            extended,
            row_anchor,
            col_anchor,
            total_rows,
            total_cols,
        )
        projected = jnp.dot(
            attended.reshape(tokens, HW), weight_o, preferred_element_type=jnp.float32
        )
        return (hidden + shift_scale[2] * projected.reshape(hidden.shape)).astype(jnp.bfloat16)

    def vacant():
        return jnp.zeros(hidden.shape, jnp.bfloat16)

    return lax.cond(active, finish, vacant)


def zero_project(control_out, weight_z):
    flattened = control_out.reshape(-1, D)
    return (
        jnp.dot(flattened, weight_z, preferred_element_type=jnp.float32)
        .astype(jnp.bfloat16)
        .reshape(control_out.shape)
    )


def on_device(latent, modulation, w_query, w_keyval, w_out, w_zero):
    sources = (w_query, w_keyval, w_out)
    weight_q, weight_kv, weight_o, weight_z = (
        lax.all_gather(sources[0], "tcol", axis=2, tiled=True),
        lax.all_gather(sources[1], "tcol", axis=2, tiled=True),
        lax.all_gather(sources[2], "tcol", axis=1, tiled=True),
        lax.all_gather(w_zero, "tcol", axis=1, tiled=True),
    )
    branch_index = lax.axis_index("branch")
    is_control = branch_index == 1
    own_copy = latent[0]
    shift_scale = lax.dynamic_index_in_dim(modulation, branch_index, 0, keepdims=False)
    received = shifted(own_copy, "branch", 1)
    control_in = own_copy.astype(jnp.float32) + received.astype(jnp.float32)
    control_out = run_block(
        is_control, control_in, shift_scale, weight_q[0], weight_kv[0], weight_o[0]
    )

    def with_projection():
        return zero_project(control_out, weight_z)

    def without_projection():
        return jnp.zeros(control_out.shape, jnp.bfloat16)

    residual = lax.cond(is_control, with_projection, without_projection)
    returned = shifted(residual, "branch", -1)
    base_in = own_copy.astype(jnp.float32) + returned.astype(jnp.float32)
    base_out = run_block(
        jnp.logical_not(is_control), base_in, shift_scale, weight_q[0], weight_kv[0], weight_o[0]
    )
    return jnp.where(is_control, control_out, base_out)[None]


def solution(mesh):
    placed = (
        P("branch", None, "trow", "tcol", None),
        P(),
        P("branch", None, "tcol"),
        P("branch", None, "tcol"),
        P("branch", "tcol", None),
        P(None, "tcol"),
    )
    return jax.shard_map(
        on_device,
        mesh=mesh,
        in_specs=placed,
        out_specs=P("branch", None, "trow", "tcol", None),
        check_vma=False,
    )
```

profile of v0, /device:TPU:1, one launch (start us, length us, event | category | flops | bytes accessed | tf_op | source)
XLA Modules:
  0.0 417.9 jit_solution(13802482478232100090)
XLA Ops:
  12.0 8.3 %collective-permute-start = (bf16[2,8,8,1152]{3,2,1,0:T(8,128)(2,1)}, bf16[2,8,8,1152]{3,2,1,0:T(8,128)(2,1)S(1)}, u32[]{:S(2)}, u32[]{:S(2)}) collective-permute-start(bf16[2,8,8,1152]{3,2,1,0:T(8,128)(2,1)} %bitcast.100), channel_id=1, source_target_pairs={{0,256},{1,257},{2,258},{3,259},{4,260},{5,261},{6,262},{7,263},{8... | collective-permute-start | bytes 884744 | tf_op jit(solution)/shard_map/ppermute | solution.py:30
  20.4 5.9 %collective-permute-done = bf16[2,8,8,1152]{3,2,1,0:T(8,128)(2,1)S(1)} collective-permute-done((bf16[2,8,8,1152]{3,2,1,0:T(8,128)(2,1)}, bf16[2,8,8,1152]{3,2,1,0:T(8,128)(2,1)S(1)}, u32[]{:S(2)}, u32[]{:S(2)}) %collective-permute-start) | collective-permute-done | bytes 294944 | tf_op jit(solution)/shard_map/ppermute | solution.py:30
  27.3 51.8 %all-gather.6.cloned.1.call-done = bf16[1,1152,576]{1,0,2:T(2,128)(2,1)} async-done(((bf16[1,1152,18]{1,0,2:T(2,128)(2,1)}), bf16[1,1152,576]{1,0,2:T(2,128)(2,1)}) %all-gather.6.cloned.1.call-update) | async-done | bytes 1327120 | tf_op jit(solution)/shard_map/all_gather | solution.py:169
  79.1 3.0 copy.120
  82.1 68.8 %all-gather.8.cloned.1.call-done = bf16[1,1152,1152]{1,0,2:T(2,128)(2,1)} async-done(((bf16[1,1152,36]{1,0,2:T(2,128)(2,1)}), bf16[1,1152,1152]{1,0,2:T(2,128)(2,1)}) %all-gather.8.cloned.1.call-update) | async-done | bytes 2654224 | tf_op jit(solution)/shard_map/all_gather | solution.py:170
  150.9 10.9 %copy.67 = bf16[1,1152,1152]{2,1,0:T(8,128)(2,1)S(1)} copy(bf16[1,1152,1152]{1,0,2:T(2,128)(2,1)} %all-gather.8.cloned.1.call-done) | data formatting | bytes 5308416 | tf_op jit(solution)/shard_map/all_gather | solution.py:170
  165.0 4.0 collective-permute-start.1
  169.0 3.3 collective-permute-done.2
  176.4 3.3 collective-permute-start.4
  181.0 2.5 collective-permute-start.3
  183.5 38.2 %all-gather.10.cloned.1.call-done = bf16[1,576,1152]{2,0,1:T(2,128)(2,1)} async-done(((bf16[1,18,1152]{2,0,1:T(2,128)(2,1)}), bf16[1,576,1152]{2,0,1:T(2,128)(2,1)}) %all-gather.10.cloned.1.call-update) | async-done | bytes 1327120 | tf_op jit(solution)/shard_map/all_gather | solution.py:171
  221.7 3.0 copy.119
  224.7 63.1 %all-gather.12.cloned.1.call-done = bf16[32,36,1152]{2,1,0:T(8,128)(2,1)} async-done(((bf16[1,36,1152]{2,1,0:T(8,128)(2,1)}), bf16[32,36,1152]{2,1,0:T(8,128)(2,1)}) %all-gather.12.cloned.1.call-update) | async-done | bytes 2654224 | tf_op jit(solution)/shard_map/all_gather | solution.py:172
  287.8 5.2 %reshape.395 = bf16[1152,1152]{1,0:T(8,128)(2,1)} reshape(bf16[32,36,1152]{2,1,0:T(8,128)(2,1)} %all-gather.12.cloned.1.call-done) | data formatting | bytes 5308416
  295.3 3.0 pad_maximum_fusion
  300.6 41.7 %collective-permute-done.5 = bf16[2,8,8,1152]{3,2,1,0:T(8,128)(2,1)} collective-permute-done((bf16[2,8,8,1152]{3,2,1,0:T(8,128)(2,1)S(1)}, bf16[2,8,8,1152]{3,2,1,0:T(8,128)(2,1)}, u32[]{:S(2)}, u32[]{:S(2)}) %collective-permute-start.5) | collective-permute-done | bytes 294944 | tf_op jit(solution)/shard_map/ppermute | solution.py:30
  343.4 3.7 conditional.8
  344.0 1.8 convolution_convert_fusion.5
  349.5 4.0 collective-permute-start.6
  353.5 2.6 collective-permute-done.7
  358.7 4.0 collective-permute-start.9
  363.2 8.5 %collective-permute-start.8 = (bf16[2,20,6,1152]{3,0,2,1:T(2,128)(2,1)S(1)}, bf16[2,20,6,1152]{3,0,2,1:T(2,128)(2,1)S(1)}, u32[]{:S(2)}, u32[]{:S(2)}) collective-permute-start(bf16[2,20,6,1152]{3,0,2,1:T(2,128)(2,1)S(1)} %copy.78), channel_id=1, source_target_pairs={{0,1},{1,2},{2,3},{3,4},{4,5},{5,6},{6,7},{7,8},{8,9},{9,10},{10,1... | collective-permute-start | bytes 1658888 | tf_op jit(solution)/shard_map/ppermute | solution.py:19
  371.7 9.8 %collective-permute-done.9 = bf16[2,20,6,1152]{3,0,2,1:T(2,128)(2,1)S(1)} collective-permute-done((bf16[2,20,6,1152]{3,0,2,1:T(2,128)(2,1)S(1)}, bf16[2,20,6,1152]{3,0,2,1:T(2,128)(2,1)S(1)}, u32[]{:S(2)}, u32[]{:S(2)}) %collective-permute-start.9) | collective-permute-done | bytes 552992 | tf_op jit(solution)/shard_map/ppermute | solution.py:22
  381.7 3.1 pad_maximum_fusion.1
  384.8 24.9 %conditional.9 = (bf16[2,8,8,1152]{3,2,1,0:T(8,128)(2,1)}) conditional(s32[]{:T(128)} %convert_element_type.76, () %tuple.47, (f32[3,1152]{1,0:T(4,128)S(1)}, bf16[2,20,20,1152]{3,2,1,0:T(8,128)(2,1)}, s32[]{:T(128)}, s32[]{:T(128)}, bf16[128,576]{0,1:T(8,128)(2,1)S(1)}, /*index=5*/bf16[576,1152]{1,0:T(8,128)(2,1)S(1)}, ...), branch_computations={%region_14.15_spmd, %region_15.18_spmd} | conditional | flops 324553312 | bytes 28789580 | solution.py:154
  384.8 3.1 copy.82
  387.9 5.6 %pad_slice_fusion.2 = (bf16[2,512,576]{2,0,1:T(2,128)(2,1)S(1)}, bf16[2,512,576]{2,0,1:T(2,128)(2,1)}) fusion(bf16[2,400,1152]{2,0,1:T(2,128)(2,1)S(1)} %bitcast.91), kind=kLoop, calls=%fused_computation.55 | loop fusion | bytes 4202496 | tf_op jit(solution)/shard_map/cond/branch_1_fun/while/body/eval_jaxpr/slice | solution.py:87
  393.5 4.2 %copy.61 = bf16[2,512,576]{1,2,0:T(8,128)(2,1)} copy(bf16[2,512,576]{2,0,1:T(2,128)(2,1)} %get-tuple-element.221) | data formatting | bytes 2359296 | tf_op jit(solution)/shard_map/cond/branch_1_fun/while/body/eval_jaxpr/slice | solution.py:88
  398.4 3.1 copy.62
  402.4 3.6 fusion.41
  406.0 2.2 fusion.24
  409.7 1.7 select_bitcast_fusion
  (81 shorter events, 32.6 us)
Async XLA Ops:
  6.5 13.8 %copy-start = (f32[2,3,1152]{2,0,1:T(2,128)S(1)}, f32[2,3,1152]{2,0,1:T(2,128)}, u32[]{:S(2)}) copy-start(f32[2,3,1152]{2,0,1:T(2,128)} %param.17) | copy-start | bytes 82948
  6.5 72.6 %all-gather.6.cloned.1.call-start = ((), (), s32[]{:S(2)}) async-start(), calls=%async_computation | async-start | bytes 2737152 | tf_op jit(solution)/shard_map/all_gather | solution.py:169
  8.1 142.8 %all-gather.8.cloned.1.call-start = ((), (), s32[]{:S(2)}) async-start(), calls=%async_computation.1 | async-start | bytes 5474304 | tf_op jit(solution)/shard_map/all_gather | solution.py:170
  9.8 211.8 %all-gather.10.cloned.1.call-start = ((), (), s32[]{:S(2)}) async-start(), calls=%async_computation.2 | async-start | bytes 2737152 | tf_op jit(solution)/shard_map/all_gather | solution.py:171
  11.4 276.4 %all-gather.12.cloned.1.call-start = ((), (), s32[]{:S(2)}) async-start(), calls=%async_computation.3 | async-start | bytes 3041280 | tf_op jit(solution)/shard_map/all_gather | solution.py:172
  12.0 14.3 %collective-permute-start = (bf16[2,8,8,1152]{3,2,1,0:T(8,128)(2,1)}, bf16[2,8,8,1152]{3,2,1,0:T(8,128)(2,1)S(1)}, u32[]{:S(2)}, u32[]{:S(2)}) collective-permute-start(bf16[2,8,8,1152]{3,2,1,0:T(8,128)(2,1)} %bitcast.100), channel_id=1, source_target_pairs={{0,256},{1,257},{2,258},{3,259},{4,260},{5,261},{6,262},{7,263},{8... | collective-permute-start | bytes 884744 | tf_op jit(solution)/shard_map/ppermute | solution.py:30
  162.6 1.1 copy-start.5
  163.7 8.6 %collective-permute-start.2 = (bf16[2,6,8,1152]{3,2,1,0:T(8,128)(2,1)S(1)}, bf16[2,6,8,1152]{3,2,1,0:T(8,128)(2,1)S(1)}, u32[]{:S(2)}, u32[]{:S(2)}) collective-permute-start(bf16[2,6,8,1152]{3,2,1,0:T(8,128)(2,1)S(1)} %get-tuple-element.235), channel_id=1, source_target_pairs={{32,0},{64,32},{96,64},{128,96},{160,128},{192,160},{224,192},{33,... | collective-permute-start | bytes 663560 | tf_op jit(solution)/shard_map/ppermute | solution.py:22
  165.0 8.2 %collective-permute-start.1 = (bf16[2,6,8,1152]{3,2,1,0:T(8,128)(2,1)S(1)}, bf16[2,6,8,1152]{3,2,1,0:T(8,128)(2,1)S(1)}, u32[]{:S(2)}, u32[]{:S(2)}) collective-permute-start(bf16[2,6,8,1152]{3,2,1,0:T(8,128)(2,1)S(1)} %get-tuple-element.234), channel_id=1, source_target_pairs={{0,32},{32,64},{64,96},{96,128},{128,160},{160,192},{192,224},{1,3... | collective-permute-start | bytes 663560 | tf_op jit(solution)/shard_map/ppermute | solution.py:19
  173.2 0.7 copy-start.3
  176.4 116.6 %collective-permute-start.4 = (bf16[2,20,6,1152]{3,0,2,1:T(2,128)(2,1)}, bf16[2,20,6,1152]{3,0,2,1:T(2,128)(2,1)}, u32[]{:S(2)}, u32[]{:S(2)}) collective-permute-start(bf16[2,20,6,1152]{3,0,2,1:T(2,128)(2,1)} %copy.70), channel_id=1, source_target_pairs={{1,0},{2,1},{3,2},{4,3},{5,4},{6,5},{7,6},{8,7},{9,8},{10,9},{11,1... | collective-permute-start | bytes 1658888 | tf_op jit(solution)/shard_map/ppermute | solution.py:22
  181.0 113.2 %collective-permute-start.3 = (bf16[2,20,6,1152]{3,0,2,1:T(2,128)(2,1)}, bf16[2,20,6,1152]{3,0,2,1:T(2,128)(2,1)}, u32[]{:S(2)}, u32[]{:S(2)}) collective-permute-start(bf16[2,20,6,1152]{3,0,2,1:T(2,128)(2,1)} %copy.69), channel_id=1, source_target_pairs={{0,1},{1,2},{2,3},{3,4},{4,5},{5,6},{6,7},{7,8},{8,9},{9,10},{10,1... | collective-permute-start | bytes 1658888 | tf_op jit(solution)/shard_map/ppermute | solution.py:19
  293.0 2.3 copy-start.4
  299.2 43.0 %collective-permute-start.5 = (bf16[2,8,8,1152]{3,2,1,0:T(8,128)(2,1)S(1)}, bf16[2,8,8,1152]{3,2,1,0:T(8,128)(2,1)}, u32[]{:S(2)}, u32[]{:S(2)}) collective-permute-start(bf16[2,8,8,1152]{3,2,1,0:T(8,128)(2,1)S(1)} %get-tuple-element.245), channel_id=1, source_target_pairs={{256,0},{257,1},{258,2},{259,3},{260,4},{261,5},{262,6},{263,7},{2... | collective-permute-start | bytes 884744 | tf_op jit(solution)/shard_map/ppermute | solution.py:30
  348.2 7.9 %collective-permute-start.7 = (bf16[2,6,8,1152]{3,2,1,0:T(8,128)(2,1)S(1)}, bf16[2,6,8,1152]{3,2,1,0:T(8,128)(2,1)S(1)}, u32[]{:S(2)}, u32[]{:S(2)}) collective-permute-start(bf16[2,6,8,1152]{3,2,1,0:T(8,128)(2,1)S(1)} %get-tuple-element.233), channel_id=1, source_target_pairs={{32,0},{64,32},{96,64},{128,96},{160,128},{192,160},{224,192},{33,... | collective-permute-start | bytes 663560 | tf_op jit(solution)/shard_map/ppermute | solution.py:22
  349.5 7.5 %collective-permute-start.6 = (bf16[2,6,8,1152]{3,2,1,0:T(8,128)(2,1)S(1)}, bf16[2,6,8,1152]{3,2,1,0:T(8,128)(2,1)S(1)}, u32[]{:S(2)}, u32[]{:S(2)}) collective-permute-start(bf16[2,6,8,1152]{3,2,1,0:T(8,128)(2,1)S(1)} %get-tuple-element.232), channel_id=1, source_target_pairs={{0,32},{32,64},{64,96},{96,128},{128,160},{160,192},{192,224},{1,3... | collective-permute-start | bytes 663560 | tf_op jit(solution)/shard_map/ppermute | solution.py:19
  358.7 22.8 %collective-permute-start.9 = (bf16[2,20,6,1152]{3,0,2,1:T(2,128)(2,1)S(1)}, bf16[2,20,6,1152]{3,0,2,1:T(2,128)(2,1)S(1)}, u32[]{:S(2)}, u32[]{:S(2)}) collective-permute-start(bf16[2,20,6,1152]{3,0,2,1:T(2,128)(2,1)S(1)} %copy.79), channel_id=1, source_target_pairs={{1,0},{2,1},{3,2},{4,3},{5,4},{6,5},{7,6},{8,7},{9,8},{10,9},{11,1... | collective-permute-start | bytes 1658888 | tf_op jit(solution)/shard_map/ppermute | solution.py:22
  363.2 18.4 %collective-permute-start.8 = (bf16[2,20,6,1152]{3,0,2,1:T(2,128)(2,1)S(1)}, bf16[2,20,6,1152]{3,0,2,1:T(2,128)(2,1)S(1)}, u32[]{:S(2)}, u32[]{:S(2)}) collective-permute-start(bf16[2,20,6,1152]{3,0,2,1:T(2,128)(2,1)S(1)} %copy.78), channel_id=1, source_target_pairs={{0,1},{1,2},{2,3},{3,4},{4,5},{5,6},{6,7},{7,8},{8,9},{9,10},{10,1... | collective-permute-start | bytes 1658888 | tf_op jit(solution)/shard_map/ppermute | solution.py:19
  381.7 3.1 copy-start.1
  384.8 8.7 %copy-start.7 = (bf16[128,576]{0,1:T(8,128)(2,1)}, bf16[128,576]{0,1:T(8,128)(2,1)S(1)}, u32[]{:S(2)}) copy-start(bf16[128,576]{0,1:T(8,128)(2,1)S(1)} %get-tuple-element.205) | copy-start | bytes 442372 | tf_op jit(solution)/shard_map/cond
  398.4 3.2 copy-start.8
  402.4 3.6 copy-start.2
Sparse Core Ops, SparseCore 0:
  9.5 69.5 all-gather.5
  81.3 69.5 all-gather.7
  153.1 68.5 all-gather.9
  223.7 64.0 all-gather.11
where the time goes:
time: 419 us; the launch traced here: 418 us
  waiting for transfers between devices  288 us (69%)
  local copies, waits for them, and re-layouts  55 us (13%)
  starting transfers between devices  38.7 us (9%)
  between operations  13.4 us (3%)
  other arithmetic  12.9 us (3%)
  matrix products  9.98 us (2%)
    all_gather x1, waiting for transfers between devices, on_device(): lax.all_gather(sources[1], 'tcol', axis=2, tiled=True)  68.8 us
    all_gather x1, waiting for transfers between devices, on_device(): lax.all_gather(w_zero, 'tcol', axis=1, tiled=True)  63.1 us
    all_gather x1, waiting for transfers between devices, on_device(): lax.all_gather(sources[0], 'tcol', axis=2, tiled=True)  51.8 us
    ppermute x2, waiting for transfers between devices, shifted(): return lax.ppermute(block, axis, route)  47.6 us
    all_gather x1, waiting for transfers between devices, on_device(): lax.all_gather(sources[2], 'tcol', axis=1, tiled=True)  38.2 us
    ppermute x4, starting transfers between devices, padded(): lax.ppermute(lax.slice_in_dim(block, block.shape[dim] - width, None, axis...  19.1 us
    unnamed x17, local copies, waits for them, and re-layouts  16.6 us
    ppermute x4, waiting for transfers between devices, padded(): lax.ppermute(lax.slice_in_dim(block, 0, width, axis=dim), axis, backward)  15.8 us
  transfers between devices with their start and end apart: 14, of which 11 were waited for; matrix products, arithmetic and copies ran while one was open for 8% of the time, Pallas kernels for 0%

commit v1 on v0

--- a/solution.py
+++ b/solution.py
@@ -168,7 +168,9 @@
     weight_q, weight_kv, weight_o, weight_z = (
         lax.all_gather(sources[0], "tcol", axis=2, tiled=True),
         lax.all_gather(sources[1], "tcol", axis=2, tiled=True),
-        lax.all_gather(sources[2], "tcol", axis=1, tiled=True),
+        jnp.concatenate(
+            lax.all_to_all(jnp.stack([sources[2]] * lax.axis_size("tcol")), "tcol", 0, 0), axis=1
+        ),
         lax.all_gather(w_zero, "tcol", axis=1, tiled=True),
     )
     branch_index = lax.axis_index("branch")

time: 419 us -> 371 us (0.89)
  waiting for transfers between devices: 288 us -> 232 us
  starting transfers between devices: 38.7 us -> 45.4 us
    all_gather x1 -> x0, waiting for transfers between devices: 38.2 us -> none  [on_device(): lax.all_gather(sources[2], 'tcol', axis=1, tiled=True)]
    all_gather x1, waiting for transfers between devices: 63.1 us -> 35.1 us  [on_device(): lax.all_gather(w_zero, 'tcol', axis=1, tiled=True)]
    all_gather x1, waiting for transfers between devices: 51.8 us -> 66.9 us  [on_device(): lax.all_gather(sources[0], 'tcol', axis=2, tiled=True)]
    ppermute x2, waiting for transfers between devices: 47.6 us -> 41.7 us  [shifted(): return lax.ppermute(block, axis, route)]
    all_to_all x0 -> x1, starting transfers between devices: none -> 5.93 us  [on_device(): lax.all_to_all(jnp.stack([sources[2]] * lax.axis_size('tcol')), 'tcol', 0...]
    another operation x5 -> x7, local copies, waits for them, and re-layouts: 4.62 us -> 10.3 us
    unnamed x17, local copies, waits for them, and re-layouts: 16.6 us -> 12.1 us
  transfers between devices with their start and end apart: 14 -> 14, of which waited for: 11 -> 9; matrix products, arithmetic and copies ran while one was open for 8% -> 9% of each run, Pallas kernels for 0% -> 0%
where the time goes in v1:
time: 371 us; the launch traced here: 369 us
  waiting for transfers between devices  232 us (63%)
  local copies, waits for them, and re-layouts  56.2 us (15%)
  starting transfers between devices  45.4 us (12%)
  between operations  13.4 us (4%)
  other arithmetic  11.9 us (3%)
  matrix products  9.95 us (3%)
    all_gather x1, waiting for transfers between devices, on_device(): lax.all_gather(sources[1], 'tcol', axis=2, tiled=True)  69.6 us
    all_gather x1, waiting for transfers between devices, on_device(): lax.all_gather(sources[0], 'tcol', axis=2, tiled=True)  66.9 us
    ppermute x2, waiting for transfers between devices, shifted(): return lax.ppermute(block, axis, route)  41.7 us
    all_gather x1, waiting for transfers between devices, on_device(): lax.all_gather(w_zero, 'tcol', axis=1, tiled=True)  35.1 us
    ppermute x4, starting transfers between devices, padded(): lax.ppermute(lax.slice_in_dim(block, block.shape[dim] - width, None, axis...  19.9 us
    ppermute x4, waiting for transfers between devices, padded(): lax.ppermute(lax.slice_in_dim(block, 0, width, axis=dim), axis, backward)  16.3 us
    unnamed x17, local copies, waits for them, and re-layouts  12.1 us
    all_gather x1, local copies, waits for them, and re-layouts, on_device(): lax.all_gather(sources[1], 'tcol', axis=2, tiled=True)  10.9 us
  transfers between devices with their start and end apart: 14, of which 9 were waited for; matrix products, arithmetic and copies ran while one was open for 9% of the time, Pallas kernels for 0%

profile of v1, /device:TPU:1, one launch (start us, length us, event | category | flops | bytes accessed | tf_op | source)
XLA Modules:
  0.0 369.1 jit_solution(7188406583961342149)
XLA Ops:
  10.6 8.3 %collective-permute-start = (bf16[2,8,8,1152]{3,2,1,0:T(8,128)(2,1)}, bf16[2,8,8,1152]{3,2,1,0:T(8,128)(2,1)S(1)}, u32[]{:S(2)}, u32[]{:S(2)}) collective-permute-start(bf16[2,8,8,1152]{3,2,1,0:T(8,128)(2,1)} %bitcast.96), channel_id=1, source_target_pairs={{0,256},{1,257},{2,258},{3,259},{4,260},{5,261},{6,262},{7,263},{8... | collective-permute-start | bytes 884744 | tf_op jit(solution)/shard_map/ppermute | solution.py:30
  18.9 2.2 stack.2
  21.1 5.9 %all-to-all-start = ((bf16[32,1,18,1152]{3,2,1,0:T(8,128)(2,1)}), bf16[32,1,18,1152]{3,2,1,0:T(8,128)(2,1)}, u32[]{:S(2)}, u32[]{:S(2)}) async-start(bf16[32,1,18,1152]{3,2,1,0:T(8,128)(2,1)} %stack.2), calls=%async_computation | async-start | bytes 3538944 | tf_op jit(solution)/shard_map/all_to_all | solution.py:172
  27.2 66.9 %all-gather.5.cloned.1.call-done = bf16[1,1152,576]{1,0,2:T(2,128)(2,1)} async-done(((bf16[1,1152,18]{1,0,2:T(2,128)(2,1)}), bf16[1,1152,576]{1,0,2:T(2,128)(2,1)}) %all-gather.5.cloned.1.call-update) | async-done | bytes 1327120 | tf_op jit(solution)/shard_map/all_gather | solution.py:169
  94.0 3.0 copy.115
  97.0 69.6 %all-gather.7.cloned.1.call-done = bf16[1,1152,1152]{1,0,2:T(2,128)(2,1)} async-done(((bf16[1,1152,36]{1,0,2:T(2,128)(2,1)}), bf16[1,1152,1152]{1,0,2:T(2,128)(2,1)}) %all-gather.7.cloned.1.call-update) | async-done | bytes 2654224 | tf_op jit(solution)/shard_map/all_gather | solution.py:170
  166.6 10.9 %copy.66 = bf16[1,1152,1152]{2,1,0:T(8,128)(2,1)S(1)} copy(bf16[1,1152,1152]{1,0,2:T(2,128)(2,1)} %all-gather.7.cloned.1.call-done) | data formatting | bytes 5308416 | tf_op jit(solution)/shard_map/all_gather | solution.py:170
  180.7 4.0 %collective-permute-start.1 = (bf16[2,6,8,1152]{3,2,1,0:T(8,128)(2,1)S(1)}, bf16[2,6,8,1152]{3,2,1,0:T(8,128)(2,1)S(1)}, u32[]{:S(2)}, u32[]{:S(2)}) collective-permute-start(bf16[2,6,8,1152]{3,2,1,0:T(8,128)(2,1)S(1)} %get-tuple-element.234), channel_id=1, source_target_pairs={{0,32},{32,64},{64,96},{96,128},{128,160},{160,192},{192,224},{1,3... | collective-permute-start | bytes 663560 | tf_op jit(solution)/shard_map/ppermute | solution.py:19
  184.8 3.3 collective-permute-done.2
  192.2 3.3 collective-permute-start.4
  196.7 2.4 collective-permute-start.3
  199.2 3.5 squeeze_reshape.4
  202.6 35.1 %all-gather.9.cloned.1.call-done = bf16[32,36,1152]{2,1,0:T(8,128)(2,1)} async-done(((bf16[1,36,1152]{2,1,0:T(8,128)(2,1)}), bf16[32,36,1152]{2,1,0:T(8,128)(2,1)}) %all-gather.9.cloned.1.call-update) | async-done | bytes 2654224 | tf_op jit(solution)/shard_map/all_gather | solution.py:174
  237.8 5.2 %reshape.398 = bf16[1152,1152]{1,0:T(8,128)(2,1)} reshape(bf16[32,36,1152]{2,1,0:T(8,128)(2,1)} %all-gather.9.cloned.1.call-done) | data formatting | bytes 5308416
  245.3 3.0 pad_maximum_fusion
  250.3 41.7 %collective-permute-done.5 = bf16[2,8,8,1152]{3,2,1,0:T(8,128)(2,1)} collective-permute-done((bf16[2,8,8,1152]{3,2,1,0:T(8,128)(2,1)S(1)}, bf16[2,8,8,1152]{3,2,1,0:T(8,128)(2,1)}, u32[]{:S(2)}, u32[]{:S(2)}) %collective-permute-start.5) | collective-permute-done | bytes 294944 | tf_op jit(solution)/shard_map/ppermute | solution.py:30
  293.1 3.7 %conditional.8 = (bf16[128,576]{0,1:T(8,128)(2,1)S(1)}, bf16[128,1152]{1,0:T(8,128)(2,1)}) conditional(s32[]{:T(128)} %convert_element_type.76, () %tuple.48, (f32[2,8,8,1152]{3,2,1,0:T(8,128)S(1)}, f32[3,1152]{1,0:T(4,128)S(1)}, bf16[1152,576]{0,1:T(8,128)(2,1)}, bf16[1152,1152]{1,0:T(8,128)(2,1)S(1)}) %tuple.107), branch_computations={%region_10.11_spmd, %region_11.14_spmd} | conditional | flops 511157504 | bytes 7110164 | solution.py:130
  293.7 1.8 convolution_convert_fusion.5
  299.2 4.0 %collective-permute-start.6 = (bf16[2,6,8,1152]{3,2,1,0:T(8,128)(2,1)S(1)}, bf16[2,6,8,1152]{3,2,1,0:T(8,128)(2,1)S(1)}, u32[]{:S(2)}, u32[]{:S(2)}) collective-permute-start(bf16[2,6,8,1152]{3,2,1,0:T(8,128)(2,1)S(1)} %get-tuple-element.232), channel_id=1, source_target_pairs={{0,32},{32,64},{64,96},{96,128},{128,160},{160,192},{192,224},{1,3... | collective-permute-start | bytes 663560 | tf_op jit(solution)/shard_map/ppermute | solution.py:19
  303.2 2.6 collective-permute-done.7
  308.4 4.0 %collective-permute-start.9 = (bf16[2,20,6,1152]{3,0,2,1:T(2,128)(2,1)S(1)}, bf16[2,20,6,1152]{3,0,2,1:T(2,128)(2,1)S(1)}, u32[]{:S(2)}, u32[]{:S(2)}) collective-permute-start(bf16[2,20,6,1152]{3,0,2,1:T(2,128)(2,1)S(1)} %copy.77), channel_id=1, source_target_pairs={{1,0},{2,1},{3,2},{4,3},{5,4},{6,5},{7,6},{8,7},{9,8},{10,9},{11,1... | collective-permute-start | bytes 1658888 | tf_op jit(solution)/shard_map/ppermute | solution.py:22
  312.9 9.5 %collective-permute-start.8 = (bf16[2,20,6,1152]{3,0,2,1:T(2,128)(2,1)S(1)}, bf16[2,20,6,1152]{3,0,2,1:T(2,128)(2,1)S(1)}, u32[]{:S(2)}, u32[]{:S(2)}) collective-permute-start(bf16[2,20,6,1152]{3,0,2,1:T(2,128)(2,1)S(1)} %copy.76), channel_id=1, source_target_pairs={{0,1},{1,2},{2,3},{3,4},{4,5},{5,6},{6,7},{7,8},{8,9},{9,10},{10,1... | collective-permute-start | bytes 1658888 | tf_op jit(solution)/shard_map/ppermute | solution.py:19
  322.4 10.3 %collective-permute-done.9 = bf16[2,20,6,1152]{3,0,2,1:T(2,128)(2,1)S(1)} collective-permute-done((bf16[2,20,6,1152]{3,0,2,1:T(2,128)(2,1)S(1)}, bf16[2,20,6,1152]{3,0,2,1:T(2,128)(2,1)S(1)}, u32[]{:S(2)}, u32[]{:S(2)}) %collective-permute-start.9) | collective-permute-done | bytes 552992 | tf_op jit(solution)/shard_map/ppermute | solution.py:22
  332.9 3.1 pad_maximum_fusion.1
  336.0 24.9 %conditional.9 = (bf16[2,8,8,1152]{3,2,1,0:T(8,128)(2,1)}) conditional(s32[]{:T(128)} %convert_element_type.76, () %tuple.47, (f32[3,1152]{1,0:T(4,128)S(1)}, bf16[2,20,20,1152]{3,2,1,0:T(8,128)(2,1)}, s32[]{:T(128)}, s32[]{:T(128)}, bf16[128,576]{0,1:T(8,128)(2,1)S(1)}, /*index=5*/bf16[576,1152]{1,0:T(8,128)(2,1)S(1)}, ...), branch_computations={%region_14.15_spmd, %region_15.18_spmd} | conditional | flops 324553312 | bytes 28789580 | solution.py:154
  336.0 3.1 copy.80
  339.1 5.6 %pad_slice_fusion.2 = (bf16[2,512,576]{2,0,1:T(2,128)(2,1)S(1)}, bf16[2,512,576]{2,0,1:T(2,128)(2,1)}) fusion(bf16[2,400,1152]{2,0,1:T(2,128)(2,1)S(1)} %bitcast.87), kind=kLoop, calls=%fused_computation.55 | loop fusion | bytes 4202496 | tf_op jit(solution)/shard_map/cond/branch_1_fun/while/body/eval_jaxpr/slice | solution.py:87
  344.7 4.2 %copy.60 = bf16[2,512,576]{1,2,0:T(8,128)(2,1)} copy(bf16[2,512,576]{2,0,1:T(2,128)(2,1)} %get-tuple-element.221) | data formatting | bytes 2359296 | tf_op jit(solution)/shard_map/cond/branch_1_fun/while/body/eval_jaxpr/slice | solution.py:88
  349.6 3.1 copy.61
  353.6 3.6 fusion.41
  357.1 2.1 fusion.24
  360.8 1.7 select_bitcast_fusion
  (82 shorter events, 30.0 us)
Async XLA Ops:
  6.5 20.5 %copy-start = (f32[2,3,1152]{2,0,1:T(2,128)S(1)}, f32[2,3,1152]{2,0,1:T(2,128)}, u32[]{:S(2)}) copy-start(f32[2,3,1152]{2,0,1:T(2,128)} %param.17) | copy-start | bytes 82948
  6.5 87.5 %all-gather.5.cloned.1.call-start = ((), (), s32[]{:S(2)}) async-start(), calls=%async_computation.1 | async-start | bytes 2737152 | tf_op jit(solution)/shard_map/all_gather | solution.py:169
  8.1 158.5 %all-gather.7.cloned.1.call-start = ((), (), s32[]{:S(2)}) async-start(), calls=%async_computation.2 | async-start | bytes 5474304 | tf_op jit(solution)/shard_map/all_gather | solution.py:170
  9.8 227.9 %all-gather.9.cloned.1.call-start = ((), (), s32[]{:S(2)}) async-start(), calls=%async_computation.3 | async-start | bytes 3041280 | tf_op jit(solution)/shard_map/all_gather | solution.py:174
  10.6 16.5 %collective-permute-start = (bf16[2,8,8,1152]{3,2,1,0:T(8,128)(2,1)}, bf16[2,8,8,1152]{3,2,1,0:T(8,128)(2,1)S(1)}, u32[]{:S(2)}, u32[]{:S(2)}) collective-permute-start(bf16[2,8,8,1152]{3,2,1,0:T(8,128)(2,1)} %bitcast.96), channel_id=1, source_target_pairs={{0,256},{1,257},{2,258},{3,259},{4,260},{5,261},{6,262},{7,263},{8... | collective-permute-start | bytes 884744 | tf_op jit(solution)/shard_map/ppermute | solution.py:30
  21.1 6.0 %copy-start.3 = (bf16[1,2,8,8,1152]{4,3,2,1,0:T(8,128)(2,1)S(1)}, bf16[1,2,8,8,1152]{4,3,2,1,0:T(8,128)(2,1)}, u32[]{:S(2)}) copy-start(bf16[1,2,8,8,1152]{4,3,2,1,0:T(8,128)(2,1)} %param.16) | copy-start | bytes 884740
  21.1 178.1 %all-to-all-start = ((bf16[32,1,18,1152]{3,2,1,0:T(8,128)(2,1)}), bf16[32,1,18,1152]{3,2,1,0:T(8,128)(2,1)}, u32[]{:S(2)}, u32[]{:S(2)}) async-start(bf16[32,1,18,1152]{3,2,1,0:T(8,128)(2,1)} %stack.2), calls=%async_computation | async-start | bytes 3538944 | tf_op jit(solution)/shard_map/all_to_all | solution.py:172
  178.3 1.1 copy-start.6
  179.4 8.6 %collective-permute-start.2 = (bf16[2,6,8,1152]{3,2,1,0:T(8,128)(2,1)S(1)}, bf16[2,6,8,1152]{3,2,1,0:T(8,128)(2,1)S(1)}, u32[]{:S(2)}, u32[]{:S(2)}) collective-permute-start(bf16[2,6,8,1152]{3,2,1,0:T(8,128)(2,1)S(1)} %get-tuple-element.235), channel_id=1, source_target_pairs={{32,0},{64,32},{96,64},{128,96},{160,128},{192,160},{224,192},{33,... | collective-permute-start | bytes 663560 | tf_op jit(solution)/shard_map/ppermute | solution.py:22
  180.7 8.2 %collective-permute-start.1 = (bf16[2,6,8,1152]{3,2,1,0:T(8,128)(2,1)S(1)}, bf16[2,6,8,1152]{3,2,1,0:T(8,128)(2,1)S(1)}, u32[]{:S(2)}, u32[]{:S(2)}) collective-permute-start(bf16[2,6,8,1152]{3,2,1,0:T(8,128)(2,1)S(1)} %get-tuple-element.234), channel_id=1, source_target_pairs={{0,32},{32,64},{64,96},{96,128},{128,160},{160,192},{192,224},{1,3... | collective-permute-start | bytes 663560 | tf_op jit(solution)/shard_map/ppermute | solution.py:19
  189.0 0.7 copy-start.4
  192.2 50.8 %collective-permute-start.4 = (bf16[2,20,6,1152]{3,0,2,1:T(2,128)(2,1)}, bf16[2,20,6,1152]{3,0,2,1:T(2,128)(2,1)}, u32[]{:S(2)}, u32[]{:S(2)}) collective-permute-start(bf16[2,20,6,1152]{3,0,2,1:T(2,128)(2,1)} %copy.69), channel_id=1, source_target_pairs={{1,0},{2,1},{3,2},{4,3},{5,4},{6,5},{7,6},{8,7},{9,8},{10,9},{11,1... | collective-permute-start | bytes 1658888 | tf_op jit(solution)/shard_map/ppermute | solution.py:22
  196.7 47.4 %collective-permute-start.3 = (bf16[2,20,6,1152]{3,0,2,1:T(2,128)(2,1)}, bf16[2,20,6,1152]{3,0,2,1:T(2,128)(2,1)}, u32[]{:S(2)}, u32[]{:S(2)}) collective-permute-start(bf16[2,20,6,1152]{3,0,2,1:T(2,128)(2,1)} %copy.68), channel_id=1, source_target_pairs={{0,1},{1,2},{2,3},{3,4},{4,5},{5,6},{6,7},{7,8},{8,9},{9,10},{10,1... | collective-permute-start | bytes 1658888 | tf_op jit(solution)/shard_map/ppermute | solution.py:19
  242.9 2.3 copy-start.5
  249.0 43.0 %collective-permute-start.5 = (bf16[2,8,8,1152]{3,2,1,0:T(8,128)(2,1)S(1)}, bf16[2,8,8,1152]{3,2,1,0:T(8,128)(2,1)}, u32[]{:S(2)}, u32[]{:S(2)}) collective-permute-start(bf16[2,8,8,1152]{3,2,1,0:T(8,128)(2,1)S(1)} %get-tuple-element.245), channel_id=1, source_target_pairs={{256,0},{257,1},{258,2},{259,3},{260,4},{261,5},{262,6},{263,7},{2... | collective-permute-start | bytes 884744 | tf_op jit(solution)/shard_map/ppermute | solution.py:30
  297.9 7.9 %collective-permute-start.7 = (bf16[2,6,8,1152]{3,2,1,0:T(8,128)(2,1)S(1)}, bf16[2,6,8,1152]{3,2,1,0:T(8,128)(2,1)S(1)}, u32[]{:S(2)}, u32[]{:S(2)}) collective-permute-start(bf16[2,6,8,1152]{3,2,1,0:T(8,128)(2,1)S(1)} %get-tuple-element.233), channel_id=1, source_target_pairs={{32,0},{64,32},{96,64},{128,96},{160,128},{192,160},{224,192},{33,... | collective-permute-start | bytes 663560 | tf_op jit(solution)/shard_map/ppermute | solution.py:22
  299.2 7.5 %collective-permute-start.6 = (bf16[2,6,8,1152]{3,2,1,0:T(8,128)(2,1)S(1)}, bf16[2,6,8,1152]{3,2,1,0:T(8,128)(2,1)S(1)}, u32[]{:S(2)}, u32[]{:S(2)}) collective-permute-start(bf16[2,6,8,1152]{3,2,1,0:T(8,128)(2,1)S(1)} %get-tuple-element.232), channel_id=1, source_target_pairs={{0,32},{32,64},{64,96},{96,128},{128,160},{160,192},{192,224},{1,3... | collective-permute-start | bytes 663560 | tf_op jit(solution)/shard_map/ppermute | solution.py:19
  308.4 24.3 %collective-permute-start.9 = (bf16[2,20,6,1152]{3,0,2,1:T(2,128)(2,1)S(1)}, bf16[2,20,6,1152]{3,0,2,1:T(2,128)(2,1)S(1)}, u32[]{:S(2)}, u32[]{:S(2)}) collective-permute-start(bf16[2,20,6,1152]{3,0,2,1:T(2,128)(2,1)S(1)} %copy.77), channel_id=1, source_target_pairs={{1,0},{2,1},{3,2},{4,3},{5,4},{6,5},{7,6},{8,7},{9,8},{10,9},{11,1... | collective-permute-start | bytes 1658888 | tf_op jit(solution)/shard_map/ppermute | solution.py:22
  312.9 19.9 %collective-permute-start.8 = (bf16[2,20,6,1152]{3,0,2,1:T(2,128)(2,1)S(1)}, bf16[2,20,6,1152]{3,0,2,1:T(2,128)(2,1)S(1)}, u32[]{:S(2)}, u32[]{:S(2)}) collective-permute-start(bf16[2,20,6,1152]{3,0,2,1:T(2,128)(2,1)S(1)} %copy.76), channel_id=1, source_target_pairs={{0,1},{1,2},{2,3},{3,4},{4,5},{5,6},{6,7},{7,8},{8,9},{9,10},{10,1... | collective-permute-start | bytes 1658888 | tf_op jit(solution)/shard_map/ppermute | solution.py:19
  332.9 3.1 copy-start.1
  336.0 8.7 %copy-start.8 = (bf16[128,576]{0,1:T(8,128)(2,1)}, bf16[128,576]{0,1:T(8,128)(2,1)S(1)}, u32[]{:S(2)}) copy-start(bf16[128,576]{0,1:T(8,128)(2,1)S(1)} %get-tuple-element.205) | copy-start | bytes 442372 | tf_op jit(solution)/shard_map/cond
  349.6 3.2 copy-start.9
  353.6 3.6 copy-start.2
Sparse Core Ops, SparseCore 0:
  9.5 84.4 all-gather.4
  96.2 70.3 all-gather.6
  168.8 68.9 all-gather.8
